TPU v7x, 32 devices: a whole 2x2x4 slice. The times are simulated.
32 devices in a mesh: groups: 2 (over x), rows: 16 (over z, y, core).
Axes of the slice: x: 2, y: 2, z: 4, core: 2. Of those that a mesh axis runs over, the one named last changes fastest.
Arguments:
- source: float32 [64, 4096], P(None, ('groups', 'rows')), parts along dimension 1, may hold values from -48 to 48
- target: float32 [64, 4096], P(None, ('groups', 'rows')), parts along dimension 1, may hold values from -48 to 48
Outputs:
- source_potential: float32 [4096], P(('groups', 'rows')), parts along dimension 0
- target_potential: float32 [4096], P(('groups', 'rows')), parts along dimension 0
- grad_source: float32 [64, 4096], P(None, ('groups', 'rows')), parts along dimension 1
- grad_target: float32 [64, 4096], P(None, ('groups', 'rows')), parts along dimension 1
There are 2 independent parts, one for each index of `groups`. A program takes and returns all parts, laid end to end along the dimension named above; each array names one. Nothing has to cross between parts.
All inputs are finite; a program needn't handle non-finite values.
Results may differ from a plain program's by a relative error of at most 0.0003.
Values sent between devices are 32-bit elements; how exact they have to be, the bound alone decides.
A program may use at most 64 MiB of HBM per device.

v0:
```python
import math

import jax
import jax.numpy as jnp
from jax import lax
from jax.sharding import PartitionSpec as P

ITERS = 4


softness = 0.2
block_width = 512


def tile_scores(left, left_sq, right, potential):
    cross = lax.dot_general(
        left,
        right,
        (((0,), (0,)), ((), ())),
        precision=lax.Precision.HIGHEST,
        preferred_element_type=jnp.float32,
    )
    right_sq = jnp.sum(right * right, axis=0)
    cost = (left_sq[:, None] + right_sq[None, :] - 2.0 * cross) / left.shape[0]
    return (potential[None, :] - cost) / softness


def absorb(running, left, left_sq, right, potential):
    scores = tile_scores(left, left_sq, right, potential)
    maxima = running[0]
    new_max = jnp.maximum(maxima, jnp.max(scores, axis=1))
    shrink = jnp.exp(maxima - new_max)
    weights = jnp.exp(scores - new_max[:, None])
    totals = running[1] * shrink + jnp.sum(weights, axis=1)
    if len(running) == 3:
        weighted = running[2] * shrink[None, :] + lax.dot_general(
            right,
            weights,
            (((1,), (1,)), ((), ())),
            precision=lax.Precision.HIGHEST,
            preferred_element_type=jnp.float32,
        )
        return (new_max, totals, weighted)
    return (new_max, totals)


def make_folder(left):
    left_sq = jnp.sum(left * left, axis=0)

    def folder(running, pieces, offset):
        right = pieces[0]
        potential = pieces[1][0]
        columns = right.shape[1]
        blocks = columns // block_width
        right_blocks = jnp.moveaxis(right.reshape(right.shape[0], blocks, block_width), 1, 0)
        pot_blocks = potential.reshape(blocks, block_width)

        def advance(inner, member):
            return (absorb(inner, left, left_sq, member[0], member[1]), None)

        running, unused = lax.scan(advance, running, (right_blocks, pot_blocks))
        return running

    return folder


def potential_of(maxima, totals, log_count):
    return -softness * (log_count + maxima + jnp.log(totals))


def column_partial(right, source, f_block):
    right_sq = jnp.sum(right * right, axis=0)
    scores = tile_scores(right, right_sq, source, f_block)
    maxima = jnp.max(scores, axis=1)
    totals = jnp.sum(jnp.exp(scores - maxima[:, None]), axis=1)
    return (maxima, totals)


def replicated_columns(source, target, f_block, log_count):
    local_count = source.shape[1]
    pieces = lax.all_gather(target, "rows", axis=1, tiled=True)
    columns = pieces.shape[1]
    blocks = columns // block_width
    right_blocks = jnp.moveaxis(pieces.reshape(pieces.shape[0], blocks, block_width), 1, 0)
    stats = lax.map(lambda member: column_partial(member, source, f_block), right_blocks)
    maxima = stats[0].reshape(columns)
    totals = stats[1].reshape(columns)
    maxima, totals = (maxima, totals)
    global_max = lax.pmax(maxima, "rows")
    summed = lax.psum(totals * jnp.exp(maxima - global_max), "rows")
    log_total = global_max + jnp.log(summed)
    g_all = -softness * (log_count + log_total)
    return lax.dynamic_slice_in_dim(g_all, lax.axis_index("rows") * local_count, local_count, 0)


def local(source, target):
    features, local_count = source.shape
    log_count = math.log(local_count * lax.axis_size("rows"))
    source_folder = make_folder(source)
    target_folder = make_folder(target)
    initial = (jnp.full((local_count,), -1e30, jnp.float32), jnp.zeros((local_count,), jnp.float32))
    with_mean = initial + (jnp.zeros((features, local_count), jnp.float32),)
    g_block = jnp.zeros((local_count,), jnp.float32)
    f_block = jnp.zeros((local_count,), jnp.float32)
    for step_index in range(ITERS):
        maxima, totals = source_folder(
            initial,
            (
                lax.all_gather(target, "rows", axis=1, tiled=True),
                lax.all_gather(g_block[None, :], "rows", axis=1, tiled=True),
            ),
            jnp.int32(0),
        )
        f_block = potential_of(maxima, totals, log_count)
        g_block = replicated_columns(source, target, f_block, log_count)
    maxima, totals, weighted = source_folder(
        with_mean,
        (
            lax.all_gather(target, "rows", axis=1, tiled=True),
            lax.all_gather(g_block[None, :], "rows", axis=1, tiled=True),
        ),
        jnp.int32(0),
    )
    row_mass = jnp.exp(f_block / softness + maxima + jnp.log(totals) + log_count)
    grad_source = row_mass[None, :] * (source - weighted / totals[None, :])
    col_max, col_totals, col_weighted = target_folder(
        with_mean,
        (
            lax.all_gather(source, "rows", axis=1, tiled=True),
            lax.all_gather(f_block[None, :], "rows", axis=1, tiled=True),
        ),
        jnp.int32(0),
    )
    grad_target = target - col_weighted / col_totals[None, :]
    return (f_block, g_block, grad_source, grad_target)


def solution(mesh):
    return jax.shard_map(
        local,
        mesh=mesh,
        in_specs=(P(None, ("groups", "rows")), P(None, ("groups", "rows"))),
        out_specs=(
            P(("groups", "rows")),
            P(("groups", "rows")),
            P(None, ("groups", "rows")),
            P(None, ("groups", "rows")),
        ),
        check_vma=False,
    )
```

profile of v0, /device:TPU:0, one launch (start us, length us, event | category | flops | bytes accessed | tf_op | source)
XLA Modules:
  0.0 419.5 jit_solution(10222245431904502799)
XLA Ops:
  1.5 24.6 %all_gather.14 = f32[64,2048]{1,0:T(8,128)S(1)} all-gather(f32[64,128]{1,0:T(8,128)S(1)} %copy-done.1), channel_id=1, replica_groups=mesh['groups'=2,'rows'=16] {'rows'}, dimensions={1}, use_global_device_ids=true | all-gather | bytes 557056 | tf_op jit(solution)/shard_map/all_gather | solution.py:109
  27.2 3.2 while.143
  30.4 2.8 while.139
  33.2 30.3 %pmax.28 = f32[2048]{0:T(1024)S(1)} all-reduce(f32[2048]{0:T(1024)S(1)} %bitcast.291), channel_id=1, replica_groups=mesh['groups'=2,'rows'=16] {'rows'}, use_global_device_ids=true, to_apply=%region_11.12 | all-reduce | flops 2048 | bytes 16384 | tf_op jit(solution)/shard_map/pmax | solution.py:89
  63.6 30.0 %psum.28 = f32[2048]{0:T(1024)S(1)} all-reduce(f32[2048]{0:T(1024)S(1)} %exponential_multiply_fusion.3), channel_id=1, replica_groups=mesh['groups'=2,'rows'=16] {'rows'}, use_global_device_ids=true, to_apply=%region_12.13 | all-reduce | flops 2048 | bytes 16384 | tf_op jit(solution)/shard_map/psum | solution.py:90
  93.7 17.0 %all-gather.5 = f32[16,1,128]{2,1,0:T(1,128)S(1)} all-gather(f32[1,1,128]{2,1,0:T(1,128)S(1)} %multiply_bitcast_fusion.2), channel_id=2, replica_groups=mesh['groups'=2,'rows'=16] {'rows'}, dimensions={0}, use_global_device_ids=true | all-gather | bytes 8704 | tf_op jit(solution)/shard_map/all_gather | solution.py:110
  111.8 3.4 while.144
  115.2 2.8 while.140
  118.0 31.9 %pmax.29 = f32[2048]{0:T(1024)S(1)} all-reduce(f32[2048]{0:T(1024)S(1)} %bitcast.293), channel_id=1, replica_groups=mesh['groups'=2,'rows'=16] {'rows'}, use_global_device_ids=true, to_apply=%region_23.24 | all-reduce | flops 2048 | bytes 16384 | tf_op jit(solution)/shard_map/pmax | solution.py:89
  149.9 30.0 %psum.29 = f32[2048]{0:T(1024)S(1)} all-reduce(f32[2048]{0:T(1024)S(1)} %exponential_multiply_fusion.2), channel_id=1, replica_groups=mesh['groups'=2,'rows'=16] {'rows'}, use_global_device_ids=true, to_apply=%region_24.25 | all-reduce | flops 2048 | bytes 16384 | tf_op jit(solution)/shard_map/psum | solution.py:90
  180.0 17.0 %all-gather.6 = f32[16,1,128]{2,1,0:T(1,128)S(1)} all-gather(f32[1,1,128]{2,1,0:T(1,128)S(1)} %multiply_bitcast_fusion.1), channel_id=3, replica_groups=mesh['groups'=2,'rows'=16] {'rows'}, dimensions={0}, use_global_device_ids=true | all-gather | bytes 8704 | tf_op jit(solution)/shard_map/all_gather | solution.py:110
  197.6 3.4 while.145
  203.8 31.9 %pmax.30 = f32[2048]{0:T(1024)S(1)} all-reduce(f32[2048]{0:T(1024)S(1)} %bitcast.295), channel_id=1, replica_groups=mesh['groups'=2,'rows'=16] {'rows'}, use_global_device_ids=true, to_apply=%region_35.36 | all-reduce | flops 2048 | bytes 16384 | tf_op jit(solution)/shard_map/pmax | solution.py:89
  235.7 30.0 %psum.30 = f32[2048]{0:T(1024)S(1)} all-reduce(f32[2048]{0:T(1024)S(1)} %exponential_multiply_fusion.1), channel_id=1, replica_groups=mesh['groups'=2,'rows'=16] {'rows'}, use_global_device_ids=true, to_apply=%region_36.37 | all-reduce | flops 2048 | bytes 16384 | tf_op jit(solution)/shard_map/psum | solution.py:90
  265.8 17.0 %all-gather.7 = f32[16,1,128]{2,1,0:T(1,128)S(1)} all-gather(f32[1,1,128]{2,1,0:T(1,128)S(1)} %multiply_bitcast_fusion), channel_id=4, replica_groups=mesh['groups'=2,'rows'=16] {'rows'}, dimensions={0}, use_global_device_ids=true | all-gather | bytes 8704 | tf_op jit(solution)/shard_map/all_gather | solution.py:110
  283.4 3.4 while.146
  286.8 2.8 while.142
  289.6 31.9 %pmax.31 = f32[2048]{0:T(1024)S(1)} all-reduce(f32[2048]{0:T(1024)S(1)} %bitcast.297), channel_id=1, replica_groups=mesh['groups'=2,'rows'=16] {'rows'}, use_global_device_ids=true, to_apply=%region_47.48 | all-reduce | flops 2048 | bytes 16384 | tf_op jit(solution)/shard_map/pmax | solution.py:89
  321.5 30.0 %psum.31 = f32[2048]{0:T(1024)S(1)} all-reduce(f32[2048]{0:T(1024)S(1)} %exponential_multiply_fusion), channel_id=1, replica_groups=mesh['groups'=2,'rows'=16] {'rows'}, use_global_device_ids=true, to_apply=%region_48.49 | all-reduce | flops 2048 | bytes 16384 | tf_op jit(solution)/shard_map/psum | solution.py:90
  352.1 17.0 %all-gather.8 = f32[16,1,128]{2,1,0:T(1,128)S(1)} all-gather(f32[1,1,128]{2,1,0:T(1,128)S(1)} %bitcast.316), channel_id=5, replica_groups=mesh['groups'=2,'rows'=16] {'rows'}, dimensions={0}, use_global_device_ids=true | all-gather | bytes 8704 | tf_op jit(solution)/shard_map/all_gather | solution.py:120
  369.7 4.6 %while.147 = (s32[]{:T(128)}, f32[128]{0:T(128)S(1)}, f32[128]{0:T(128)S(1)}, f32[64,128]{1,0:T(8,128)S(1)}, f32[4,512]{1,0:T(4,128)S(1)}, /*index=5*/f32[128]{0...) while((s32[]{:T(128)}, f32[128]{0:T(128)S(1)}, ...), condition=%wide.region_53.54_spmd.clone, body=%wide.region_49.53_spmd.clone.sunk | while | flops 101408896 | bytes 1297033 | solution.py:61
  375.1 19.0 %all-gather.9 = f32[16,1,128]{2,1,0:T(1,128)S(1)} all-gather(f32[1,1,128]{2,1,0:T(1,128)S(1)} %bitcast.317), channel_id=6, replica_groups=mesh['groups'=2,'rows'=16] {'rows'}, dimensions={0}, use_global_device_ids=true | all-gather | bytes 8704 | tf_op jit(solution)/shard_map/all_gather | solution.py:130
  394.6 18.8 %all_gather.36 = f32[64,2048]{1,0:T(8,128)S(1)} all-gather(f32[64,128]{1,0:T(8,128)S(1)} %get-tuple-element.1822), channel_id=1, replica_groups=mesh['groups'=2,'rows'=16] {'rows'}, dimensions={1}, use_global_device_ids=true | all-gather | bytes 557056 | tf_op jit(solution)/shard_map/all_gather | solution.py:129
  413.8 5.1 %while.148 = (s32[]{:T(128)}, f32[128]{0:T(128)S(1)}, f32[128]{0:T(128)S(1)}, f32[64,128]{1,0:T(8,128)S(1)}, f32[4,512]{1,0:T(4,128)S(1)}, /*index=5*/f32[128]{0...) while((s32[]{:T(128)}, f32[128]{0:T(128)S(1)}, ...), condition=%wide.region_59.60_spmd.clone, body=%wide.region_55.59_spmd.clone.sunk | while | flops 101408896 | bytes 1559169 | solution.py:61
  (326 shorter events, 43.4 us)
Async XLA Ops:
  0.6 0.9 copy-start.1
  26.4 0.8 copy-start
  289.6 85.5 %copy-start.3 = (f32[128]{0:T(128)}, f32[128]{0:T(128)S(1)}, u32[]{:S(2)}) copy-start(f32[128]{0:T(128)S(1)} %get-tuple-element.1832) | copy-start | bytes 1540
  351.6 0.5 copy-start.2
where the time goes:
time: 420 us
  blocking collectives  376 us (90%)
  matrix products  25.4 us (6%)
  other arithmetic  10.4 us (2%)
  local copies, waits for them, and re-layouts  4.82 us (1%)
    pmax x4, blocking collectives, replicated_columns(): global_max = lax.pmax(maxima, 'rows')  126 us
    psum x4, blocking collectives, replicated_columns(): summed = lax.psum(totals * jnp.exp(maxima - global_max), 'rows')  120 us
    all_gather x4, blocking collectives, local(): lax.all_gather(g_block[None, :], 'rows', axis=1, tiled=True)  68.1 us
    all_gather x1, blocking collectives, local(): lax.all_gather(target, 'rows', axis=1, tiled=True)  24.6 us
    dot_general x40, matrix products, tile_scores(): lax.dot_general(left, right, (((0,), (0,)), ((), ())), precision=lax.Prec...  22.9 us
    all_gather x1, blocking collectives, local(): lax.all_gather(f_block[None, :], 'rows', axis=1, tiled=True)  19 us
    all_gather x1, blocking collectives, local(): lax.all_gather(source, 'rows', axis=1, tiled=True)  18.8 us

commit v1 on v0

v1 whole, which is shorter than its diff:
```python
import functools
import math

import jax
import jax.numpy as jnp
from jax import lax
from jax.experimental import pallas as pl
from jax.experimental.pallas import tpu as pltpu
from jax.sharding import PartitionSpec as P

ITERS = 4
SOFTNESS = 0.2
LN2 = math.log(2.0)
HIGHEST = lax.Precision.HIGHEST
MESH = pl.DeviceIdType.MESH


def split(rows):
    src = 1
    while (src * 2) ** 2 <= rows and rows % (src * 2) == 0:
        src *= 2
    return src, rows // src


def lse2(stack):
    top = jnp.max(stack, axis=0)
    return top + jnp.log2(jnp.sum(jnp.exp2(stack - top[None]), axis=0))


def kernel(
    src,
    tgt,
    s_hbm,
    t_hbm,
    f_ref,
    g_ref,
    gs_ref,
    gt_ref,
    s_all,
    t_all,
    cross,
    weights,
    f_out,
    f_in,
    g_out,
    g_in,
    u_out,
    u_in,
    w_out,
    w_in,
    local_sem,
    point_send,
    point_recv,
    f_send,
    f_recv,
    g_send,
    g_recv,
    u_send,
    u_recv,
    w_send,
    w_recv,
):
    feats, n = s_hbm.shape
    rank = lax.axis_index("rows")
    b = lax.rem(rank, src)
    a = lax.div(rank, src)
    log_count = math.log2(n * src * tgt)
    scale = 1.0 / (feats * SOFTNESS * LN2)

    def src_peer(k):
        return {"rows": a * src + lax.rem(b + k, src)}

    def tgt_peer(k):
        return {"rows": lax.rem(a + k, tgt) * src + b}

    local_s = pltpu.make_async_copy(s_hbm, s_all.at[0], local_sem.at[0])
    local_t = pltpu.make_async_copy(t_hbm, t_all.at[0], local_sem.at[1])
    local_s.start()
    local_t.start()

    barrier = pltpu.get_barrier_semaphore()
    for k in range(1, src):
        pl.semaphore_signal(barrier, inc=1, device_id=src_peer(k), device_id_type=MESH)
    for k in range(1, tgt):
        pl.semaphore_signal(barrier, inc=1, device_id=tgt_peer(k), device_id_type=MESH)
    pl.semaphore_wait(barrier, src + tgt - 2)

    pending = []

    def send(source, target, send_sem, recv_sem, peer):
        copy = pltpu.make_async_remote_copy(
            src_ref=source, dst_ref=target, send_sem=send_sem, recv_sem=recv_sem, device_id=peer, device_id_type=MESH
        )
        copy.start()
        pending.append(copy)
        return copy

    t_copies, s_copies = {}, {}
    for k in range(max(src, tgt) - 1, 0, -1):
        if k < tgt:
            t_copies[k] = send(t_hbm, t_all.at[k], point_send.at[1, k], point_recv.at[1, k], tgt_peer(k))
        if k < src:
            s_copies[k] = send(s_hbm, s_all.at[k], point_send.at[0, k], point_recv.at[0, k], src_peer(k))

    eye = lax.broadcasted_iota(jnp.int32, (n, n), 0) == lax.broadcasted_iota(jnp.int32, (n, n), 1)

    def to_row(col):
        return jnp.sum(jnp.where(eye, jnp.broadcast_to(col, (n, n)), 0.0), axis=0, keepdims=True)

    def to_col(row):
        return jnp.sum(jnp.where(eye, jnp.broadcast_to(row, (n, n)), 0.0), axis=1, keepdims=True)

    local_s.wait()
    local_t.wait()
    for k in range(1, src):
        s_copies[k].wait_recv()
    lefts = jnp.concatenate([(s_all[p] * (2.0 * scale)).T for p in range(src)], axis=0)
    g_rows = []
    for q in range(tgt):
        if q:
            t_copies[q].wait_recv()
        t = t_all[q]
        g_rows.append(-scale * jnp.sum(t * t, axis=0, keepdims=True))
        cross[:, q * n : (q + 1) * n] = jnp.dot(lefts, t, precision=HIGHEST, preferred_element_type=jnp.float32)

    def row_weights(p, g_row):
        x = cross[p * n : (p + 1) * n, :] + g_row
        top = jnp.max(x, axis=1, keepdims=True)
        w = jnp.exp2(x - top)
        return top, w, jnp.sum(w, axis=1, keepdims=True)

    f_hat = None
    g_hat = None
    for it in range(ITERS):
        last = it == ITERS - 1
        g_row = jnp.concatenate(g_rows, axis=1)
        for p in range(src):
            top, w, total = row_weights(p, g_row)
            part = to_row(top + jnp.log2(total))
            f_out[it, p] = part
            f_out[it, src + p] = part
            f_in[it, 0, p] = part
        copies = [
            send(f_out.at[it, pl.ds(src - k, src)], f_in.at[it, k], f_send.at[it, k], f_recv.at[it, k], src_peer(k))
            for k in range(1, src)
        ]
        for copy in copies:
            copy.wait_recv()
        f_hat = -(log_count + lse2(f_in[it]))
        cols = [to_col(f_hat[p]) for p in range(src)]
        top = None
        for p in range(src):
            piece = jnp.max(cross[p * n : (p + 1) * n, :] + cols[p], axis=0, keepdims=True)
            top = piece if top is None else jnp.maximum(top, piece)
        total = None
        for p in range(src):
            w = jnp.exp2((cross[p * n : (p + 1) * n, :] + cols[p]) - top)
            if last:
                weights[p * n : (p + 1) * n, :] = w
            piece = jnp.sum(w, axis=0, keepdims=True)
            total = piece if total is None else total + piece
        part = top + jnp.log2(total)
        for q in range(tgt):
            piece = part[:, q * n : (q + 1) * n]
            g_out[it, q] = piece
            g_out[it, tgt + q] = piece
            g_in[it, 0, q] = piece
        copies = [
            send(g_out.at[it, pl.ds(tgt - k, tgt)], g_in.at[it, k], g_send.at[it, k], g_recv.at[it, k], tgt_peer(k))
            for k in range(1, tgt)
        ]
        if last:
            means = jnp.dot(
                jnp.concatenate([s_all[p] for p in range(src)], axis=1),
                weights[...],
                precision=HIGHEST,
                preferred_element_type=jnp.float32,
            ) * (1.0 / total)
            for q in range(tgt):
                u_out[q] = means[:, q * n : (q + 1) * n]
            u_copies = [
                send(u_out.at[q], u_in.at[q], u_send.at[q], u_recv.at[q], tgt_peer(tgt - q)) for q in range(1, tgt)
            ]
        for copy in copies:
            copy.wait_recv()
        g_hat = -(log_count + lse2(g_in[it]))
        g_rows = [g_hat[q] for q in range(tgt)]

    g_row = jnp.concatenate(g_rows, axis=1)
    rights = jnp.concatenate([t_all[q] for q in range(tgt)], axis=1)
    w_copies = []
    for p in list(range(1, src)) + [0]:
        top, w, total = row_weights(p, g_row)
        mean = lax.dot_general(
            rights, w, (((1,), (1,)), ((), ())), precision=HIGHEST, preferred_element_type=jnp.float32
        )
        w_out[p, :feats, :] = mean * to_row(1.0 / total)
        w_out[p, feats:, :] = jnp.broadcast_to(to_row(top + jnp.log2(total)), (8, n))
        if p:
            w_copies.append(send(w_out.at[p], w_in.at[p], w_send.at[p], w_recv.at[p], src_peer(src - p)))

    s = s_all[0]
    t = t_all[0]
    f_ref[...] = (f_hat[0] + scale * jnp.sum(s * s, axis=0, keepdims=True)) * (SOFTNESS * LN2)
    g_ref[...] = (g_hat[0] + scale * jnp.sum(t * t, axis=0, keepdims=True)) * (SOFTNESS * LN2)

    for copy in u_copies:
        copy.wait_recv()
    col_lse = -(g_hat[0] + log_count)
    mean = u_out[0] * jnp.exp2(g_in[ITERS - 1, 0, 0] - col_lse)
    for q in range(1, tgt):
        mean = mean + u_in[q] * jnp.exp2(g_in[ITERS - 1, tgt - q, 0] - col_lse)
    gt_ref[...] = t - mean

    for copy in w_copies:
        copy.wait_recv()
    parts = [w_out[0, feats : feats + 1, :]] + [w_in[p, feats : feats + 1, :] for p in range(1, src)]
    row_lse = lse2(jnp.stack(parts))
    mean = w_out[0, :feats, :] * jnp.exp2(parts[0] - row_lse)
    for p in range(1, src):
        mean = mean + w_in[p, :feats, :] * jnp.exp2(parts[p] - row_lse)
    gs_ref[...] = jnp.exp2(f_hat[0] + row_lse + log_count) * (s - mean)

    for copy in pending:
        copy.wait_send()


def solution(mesh):
    src, tgt = split(mesh.shape["rows"])

    def local(source, target):
        feats, n = source.shape
        f32 = jnp.float32
        dma = pltpu.SemaphoreType.DMA
        row = jax.ShapeDtypeStruct((1, n), f32)
        block = jax.ShapeDtypeStruct((feats, n), f32)
        f, g, gs, gt = pl.pallas_call(
            functools.partial(kernel, src, tgt),
            out_shape=(row, row, block, block),
            in_specs=[pl.BlockSpec(memory_space=pl.ANY)] * 2,
            out_specs=tuple([pl.BlockSpec(memory_space=pltpu.VMEM)] * 4),
            scratch_shapes=[
                pltpu.VMEM((src, feats, n), f32),
                pltpu.VMEM((tgt, feats, n), f32),
                pltpu.VMEM((src * n, tgt * n), f32),
                pltpu.VMEM((src * n, tgt * n), f32),
                pltpu.VMEM((ITERS, 2 * src, 1, n), f32),
                pltpu.VMEM((ITERS, src, src, 1, n), f32),
                pltpu.VMEM((ITERS, 2 * tgt, 1, n), f32),
                pltpu.VMEM((ITERS, tgt, tgt, 1, n), f32),
                pltpu.VMEM((tgt, feats, n), f32),
                pltpu.VMEM((tgt, feats, n), f32),
                pltpu.VMEM((src, feats + 8, n), f32),
                pltpu.VMEM((src, feats + 8, n), f32),
                dma((2,)),
                dma((2, max(src, tgt))),
                dma((2, max(src, tgt))),
                dma((ITERS, src)),
                dma((ITERS, src)),
                dma((ITERS, tgt)),
                dma((ITERS, tgt)),
                dma((tgt,)),
                dma((tgt,)),
                dma((src,)),
                dma((src,)),
            ],
            compiler_params=pltpu.CompilerParams(
                collective_id=0, has_side_effects=True, vmem_limit_bytes=48 * 1024 * 1024
            ),
        )(source, target)
        return f.reshape(n), g.reshape(n), gs, gt

    spec = P(("groups", "rows"))
    wide = P(None, ("groups", "rows"))
    return jax.shard_map(
        local, mesh=mesh, in_specs=(wide, wide), out_specs=(spec, spec, wide, wide), check_vma=False
    )
```

time: 420 us -> 47.7 us (0.11)
  blocking collectives: 376 us -> 0 us
  Pallas kernels: 0 us -> 43 us
  matrix products: 25.4 us -> 0 us
  other arithmetic: 10.4 us -> 0 us
    all_gather x7 -> x0, blocking collectives: 130 us -> none  [the longest x4 68.1 us: local(): lax.all_gather(g_block[None, :], 'rows', axis=1, tiled=True)]
    pmax x4 -> x0, blocking collectives: 126 us -> none  [replicated_columns(): global_max = lax.pmax(maxima, 'rows')]
    psum x4 -> x0, blocking collectives: 120 us -> none  [replicated_columns(): summed = lax.psum(totals * jnp.exp(maxima - global_max), 'rows')]
    pallas_call x0 -> x1, Pallas kernels: none -> 43 us  [local(): pl.pallas_call(functools.partial(kernel, src, tgt), out_shape=(row, row,...]
    dot_general x48 -> x0, matrix products: 25.4 us -> none  [the longest x40 22.9 us: tile_scores(): lax.dot_general(left, right, (((0,), (0,)), ((), ())), precision=lax.Prec...]
    reduce_sum x82 -> x0, other arithmetic: 5.32 us -> none  [the longest x24 2.2 us: absorb(): totals = running[1] * shrink + jnp.sum(weights, axis=1)]
where the time goes in v1:
time: 47.7 us; the launch traced here: 47.4 us
  Pallas kernels  43 us (90%)
  local copies, waits for them, and re-layouts  3.76 us (8%)
  between operations  0.65 us (1%)
    pallas_call x1, Pallas kernels, local(): pl.pallas_call(functools.partial(kernel, src, tgt), out_shape=(row, row,...  43 us
    unnamed x8, local copies, waits for them, and re-layouts  3.76 us

profile of v1, /device:TPU:0, one launch (start us, length us, event | category | flops | bytes accessed | tf_op | source)
XLA Modules:
  0.0 47.4 jit_solution(16899519842004174843)
XLA Ops:
  0.6 0.0 copy-start
  0.6 0.7 %copy-done = f32[64,128]{1,0:T(8,128)S(1)} copy-done((f32[64,128]{1,0:T(8,128)S(1)}, f32[64,128]{1,0:T(8,128)}, u32[]{:S(2)}) %copy-start) | copy-done | bytes 32792
  1.4 0.0 copy-start.1
  1.4 0.8 %copy-done.1 = f32[64,128]{1,0:T(8,128)S(1)} copy-done((f32[64,128]{1,0:T(8,128)S(1)}, f32[64,128]{1,0:T(8,128)}, u32[]{:S(2)}) %copy-start.1) | copy-done | bytes 32792
  2.1 43.0 %shard_map.57 = (f32[1,128]{1,0:T(1,128)S(1)}, f32[1,128]{1,0:T(1,128)S(1)}, f32[64,128]{1,0:T(8,128)S(1)}, f32[64,128]{1,0:T(8,128)S(1)}) custom-call(f32[64,128]{1,0:T(8,128)S(1)} %copy-done, f32[64,128]{1,0:T(8,128)S(1)} %copy-done.1), custom_call_target="tpu_custom_call" | custom-call | tf_op jit(solution)/shard_map/pallas_call | solution.py:237
  45.2 0.5 %copy.10 = f32[128]{0:T(128)} copy(f32[128]{0:T(128)S(1)} %bitcast.3) | data formatting | bytes 1024
  45.7 0.5 %copy.11 = f32[128]{0:T(128)} copy(f32[128]{0:T(128)S(1)} %bitcast.2) | data formatting | bytes 1024
  46.2 0.6 %copy.12 = f32[64,128]{1,0:T(8,128)} copy(f32[64,128]{1,0:T(8,128)S(1)} %get-tuple-element.18) | data formatting | bytes 65536
  46.8 0.6 %copy.13 = f32[64,128]{1,0:T(8,128)} copy(f32[64,128]{1,0:T(8,128)S(1)} %get-tuple-element.19) | data formatting | bytes 65536
Async XLA Ops:
  0.6 0.8 %copy-start = (f32[64,128]{1,0:T(8,128)S(1)}, f32[64,128]{1,0:T(8,128)}, u32[]{:S(2)}) copy-start(f32[64,128]{1,0:T(8,128)} %s_hbm.1) | copy-start | bytes 98308
  1.4 0.8 %copy-start.1 = (f32[64,128]{1,0:T(8,128)S(1)}, f32[64,128]{1,0:T(8,128)}, u32[]{:S(2)}) copy-start(f32[64,128]{1,0:T(8,128)} %t_hbm.1) | copy-start | bytes 98308

commit v2 on v1

--- a/solution.py
+++ b/solution.py
@@ -16,9 +16,7 @@
 
 
 def split(rows):
-    src = 1
-    while (src * 2) ** 2 <= rows and rows % (src * 2) == 0:
-        src *= 2
+    src = 2 if rows % 2 == 0 else 1
     return src, rows // src
 
 
@@ -39,13 +37,12 @@
     s_all,
     t_all,
     cross,
-    weights,
+    own_cross,
     f_out,
     f_in,
+    f_all,
     g_out,
     g_in,
-    u_out,
-    u_in,
     w_out,
     w_in,
     local_sem,
@@ -55,8 +52,10 @@
     f_recv,
     g_send,
     g_recv,
-    u_send,
-    u_recv,
+    b_send,
+    b_recv,
+    h_send,
+    h_recv,
     w_send,
     w_recv,
 ):
@@ -73,7 +72,7 @@
     def tgt_peer(k):
         return {"rows": lax.rem(a + k, tgt) * src + b}
 
-    local_s = pltpu.make_async_copy(s_hbm, s_all.at[0], local_sem.at[0])
+    local_s = pltpu.make_async_copy(s_hbm, s_all.at[0, 0], local_sem.at[0])
     local_t = pltpu.make_async_copy(t_hbm, t_all.at[0], local_sem.at[1])
     local_s.start()
     local_t.start()
@@ -100,7 +99,7 @@
         if k < tgt:
             t_copies[k] = send(t_hbm, t_all.at[k], point_send.at[1, k], point_recv.at[1, k], tgt_peer(k))
         if k < src:
-            s_copies[k] = send(s_hbm, s_all.at[k], point_send.at[0, k], point_recv.at[0, k], src_peer(k))
+            s_copies[k] = send(s_hbm, s_all.at[k, 0], point_send.at[0, k], point_recv.at[0, k], src_peer(k))
 
     eye = lax.broadcasted_iota(jnp.int32, (n, n), 0) == lax.broadcasted_iota(jnp.int32, (n, n), 1)
 
@@ -114,7 +113,7 @@
     local_t.wait()
     for k in range(1, src):
         s_copies[k].wait_recv()
-    lefts = jnp.concatenate([(s_all[p] * (2.0 * scale)).T for p in range(src)], axis=0)
+    lefts = jnp.concatenate([(s_all[p, 0] * (2.0 * scale)).T for p in range(src)], axis=0)
     g_rows = []
     for q in range(tgt):
         if q:
@@ -129,36 +128,61 @@
         w = jnp.exp2(x - top)
         return top, w, jnp.sum(w, axis=1, keepdims=True)
 
+    own_left = (t_all[0] * (2.0 * scale)).T
+
+    def own_columns(p, k):
+        slot = p * tgt + k
+        own_cross[:, slot * n : (slot + 1) * n] = jnp.dot(
+            own_left, s_all[p, k], precision=HIGHEST, preferred_element_type=jnp.float32
+        )
+
+    batches = [list(range(1, tgt))[i :: ITERS - 1] for i in range(ITERS - 1)]
+    arriving, handed = {}, []
     f_hat = None
     g_hat = None
     for it in range(ITERS):
         last = it == ITERS - 1
+        if it:
+            for k in batches[it - 1]:
+                arriving[k].wait_recv()
+                for p in range(1, src):
+                    handed.append(
+                        (p, k, send(s_all.at[0, k], s_all.at[p, k], h_send.at[p, k], h_recv.at[p, k], src_peer(p)))
+                    )
+        if not last:
+            for k in batches[it]:
+                arriving[k] = send(s_hbm, s_all.at[0, k], b_send.at[k], b_recv.at[k], tgt_peer(k))
         g_row = jnp.concatenate(g_rows, axis=1)
+        copies = []
         for p in range(src):
             top, w, total = row_weights(p, g_row)
             part = to_row(top + jnp.log2(total))
             f_out[it, p] = part
-            f_out[it, src + p] = part
-            f_in[it, 0, p] = part
-        copies = [
-            send(f_out.at[it, pl.ds(src - k, src)], f_in.at[it, k], f_send.at[it, k], f_recv.at[it, k], src_peer(k))
-            for k in range(1, src)
-        ]
-        for copy in copies:
-            copy.wait_recv()
-        f_hat = -(log_count + lse2(f_in[it]))
-        cols = [to_col(f_hat[p]) for p in range(src)]
-        top = None
+            f_in[it, p, 0] = part
+            for k in range(1, src):
+                to = (p + k) % src
+                copies.append(
+                    (to, send(f_out.at[it, p], f_in.at[it, to, k], f_send.at[it, to, k], f_recv.at[it, to, k], src_peer(k)))
+                )
+        f_hat = []
+        tops, totals = [], []
         for p in range(src):
-            piece = jnp.max(cross[p * n : (p + 1) * n, :] + cols[p], axis=0, keepdims=True)
-            top = piece if top is None else jnp.maximum(top, piece)
-        total = None
-        for p in range(src):
-            w = jnp.exp2((cross[p * n : (p + 1) * n, :] + cols[p]) - top)
+            for to, copy in copies:
+                if to == p:
+                    copy.wait_recv()
+            f_hat.append(-(log_count + lse2(f_in[it, p])))
             if last:
-                weights[p * n : (p + 1) * n, :] = w
-            piece = jnp.sum(w, axis=0, keepdims=True)
-            total = piece if total is None else total + piece
+                f_all[0, p] = f_hat[p]
+            x = cross[p * n : (p + 1) * n, :] + to_col(f_hat[p])
+            tops.append(jnp.max(x, axis=0, keepdims=True))
+            totals.append(jnp.sum(jnp.exp2(x - tops[p]), axis=0, keepdims=True))
+        if last:
+            f_copies = [
+                send(f_all.at[0], f_all.at[k], b_send.at[tgt + k], b_recv.at[tgt + k], tgt_peer(k))
+                for k in range(1, tgt)
+            ]
+        top = functools.reduce(jnp.maximum, tops)
+        total = sum(totals[p] * jnp.exp2(tops[p] - top) for p in range(src))
         part = top + jnp.log2(total)
         for q in range(tgt):
             piece = part[:, q * n : (q + 1) * n]
@@ -169,18 +193,16 @@
             send(g_out.at[it, pl.ds(tgt - k, tgt)], g_in.at[it, k], g_send.at[it, k], g_recv.at[it, k], tgt_peer(k))
             for k in range(1, tgt)
         ]
+        if it == 0:
+            for p in range(src):
+                own_columns(p, 0)
+        else:
+            for k in batches[it - 1]:
+                own_columns(0, k)
         if last:
-            means = jnp.dot(
-                jnp.concatenate([s_all[p] for p in range(src)], axis=1),
-                weights[...],
-                precision=HIGHEST,
-                preferred_element_type=jnp.float32,
-            ) * (1.0 / total)
-            for q in range(tgt):
-                u_out[q] = means[:, q * n : (q + 1) * n]
-            u_copies = [
-                send(u_out.at[q], u_in.at[q], u_send.at[q], u_recv.at[q], tgt_peer(tgt - q)) for q in range(1, tgt)
-            ]
+            for p, k, copy in handed:
+                copy.wait_recv()
+                own_columns(p, k)
         for copy in copies:
             copy.wait_recv()
         g_hat = -(log_count + lse2(g_in[it]))
@@ -199,17 +221,23 @@
         if p:
             w_copies.append(send(w_out.at[p], w_in.at[p], w_send.at[p], w_recv.at[p], src_peer(src - p)))
 
-    s = s_all[0]
+    s = s_all[0, 0]
     t = t_all[0]
     f_ref[...] = (f_hat[0] + scale * jnp.sum(s * s, axis=0, keepdims=True)) * (SOFTNESS * LN2)
     g_ref[...] = (g_hat[0] + scale * jnp.sum(t * t, axis=0, keepdims=True)) * (SOFTNESS * LN2)
 
-    for copy in u_copies:
+    for copy in f_copies:
         copy.wait_recv()
-    col_lse = -(g_hat[0] + log_count)
-    mean = u_out[0] * jnp.exp2(g_in[ITERS - 1, 0, 0] - col_lse)
-    for q in range(1, tgt):
-        mean = mean + u_in[q] * jnp.exp2(g_in[ITERS - 1, tgt - q, 0] - col_lse)
+    slots = [(p, k) for p in range(src) for k in range(tgt)]
+    f_row = jnp.concatenate([f_all[k, p] for p, k in slots], axis=1)
+    w = jnp.exp2(own_cross[...] + f_row + to_col(g_hat[0] + log_count))
+    mean = lax.dot_general(
+        jnp.concatenate([s_all[p, k] for p, k in slots], axis=1),
+        w,
+        (((1,), (1,)), ((), ())),
+        precision=HIGHEST,
+        preferred_element_type=jnp.float32,
+    )
     gt_ref[...] = t - mean
 
     for copy in w_copies:
@@ -223,6 +251,12 @@
 
     for copy in pending:
         copy.wait_send()
+
+
+def hand_out(*refs):
+    half = len(refs) // 2
+    for x, y in zip(refs[:half], refs[half:]):
+        y[...] = x[...]
 
 
 def solution(mesh):
@@ -237,37 +271,39 @@
         f, g, gs, gt = pl.pallas_call(
             functools.partial(kernel, src, tgt),
             out_shape=(row, row, block, block),
-            in_specs=[pl.BlockSpec(memory_space=pl.ANY)] * 2,
+            in_specs=[pl.BlockSpec(memory_space=pltpu.HBM)] * 2,
             out_specs=tuple([pl.BlockSpec(memory_space=pltpu.VMEM)] * 4),
             scratch_shapes=[
-                pltpu.VMEM((src, feats, n), f32),
+                pltpu.VMEM((src, tgt, feats, n), f32),
                 pltpu.VMEM((tgt, feats, n), f32),
                 pltpu.VMEM((src * n, tgt * n), f32),
-                pltpu.VMEM((src * n, tgt * n), f32),
-                pltpu.VMEM((ITERS, 2 * src, 1, n), f32),
+                pltpu.VMEM((n, src * tgt * n), f32),
+                pltpu.VMEM((ITERS, src, 1, n), f32),
                 pltpu.VMEM((ITERS, src, src, 1, n), f32),
+                pltpu.VMEM((tgt, src, 1, n), f32),
                 pltpu.VMEM((ITERS, 2 * tgt, 1, n), f32),
                 pltpu.VMEM((ITERS, tgt, tgt, 1, n), f32),
-                pltpu.VMEM((tgt, feats, n), f32),
-                pltpu.VMEM((tgt, feats, n), f32),
                 pltpu.VMEM((src, feats + 8, n), f32),
                 pltpu.VMEM((src, feats + 8, n), f32),
                 dma((2,)),
                 dma((2, max(src, tgt))),
                 dma((2, max(src, tgt))),
-                dma((ITERS, src)),
-                dma((ITERS, src)),
+                dma((ITERS, src, src)),
+                dma((ITERS, src, src)),
                 dma((ITERS, tgt)),
                 dma((ITERS, tgt)),
-                dma((tgt,)),
-                dma((tgt,)),
+                dma((2 * tgt,)),
+                dma((2 * tgt,)),
+                dma((src, tgt)),
+                dma((src, tgt)),
                 dma((src,)),
                 dma((src,)),
             ],
             compiler_params=pltpu.CompilerParams(
-                collective_id=0, has_side_effects=True, vmem_limit_bytes=48 * 1024 * 1024
+                collective_id=0, has_side_effects=True, vmem_limit_bytes=56 * 1024 * 1024
             ),
         )(source, target)
+        f, g, gs, gt = pl.pallas_call(hand_out, out_shape=(row, row, block, block))(f, g, gs, gt)
         return f.reshape(n), g.reshape(n), gs, gt
 
     spec = P(("groups", "rows"))

time: 47.7 us -> 44.8 us (0.939)
  local copies, waits for them, and re-layouts: 3.76 us -> 0 us
  Pallas kernels: 43 us -> 43.9 us
    unnamed x8 -> x0, local copies, waits for them, and re-layouts: 3.76 us -> none
    pallas_call x0 -> x1, Pallas kernels: none -> 1.42 us  [local(): pl.pallas_call(hand_out, out_shape=(row, row, block, block))(f, g, gs, gt)]
    pallas_call x1, Pallas kernels: 43 us -> 42.5 us  [local(): pl.pallas_call(functools.partial(kernel, src, tgt), out_shape=(row, row,...]
where the time goes in v2:
time: 44.8 us; the launch traced here: 44.6 us
  Pallas kernels  43.9 us (98%)
  between operations  0.64 us (1%)
    pallas_call x1, Pallas kernels, local(): pl.pallas_call(functools.partial(kernel, src, tgt), out_shape=(row, row,...  42.5 us
    pallas_call x1, Pallas kernels, local(): pl.pallas_call(hand_out, out_shape=(row, row, block, block))(f, g, gs, gt)  1.42 us

profile of v2, /device:TPU:0, one launch (start us, length us, event | category | flops | bytes accessed | tf_op | source)
XLA Modules:
  0.0 44.6 jit_solution(7363494103681756540)
XLA Ops:
  0.6 42.5 %shard_map.57 = (f32[1,128]{1,0:T(1,128)}, f32[1,128]{1,0:T(1,128)}, f32[64,128]{1,0:T(8,128)}, f32[64,128]{1,0:T(8,128)}) custom-call(f32[64,128]{1,0:T(8,128)} %s_hbm.1, f32[64,128]{1,0:T(8,128)} %t_hbm.1), custom_call_target="tpu_custom_call" | custom-call | tf_op jit(solution)/shard_map/pallas_call | solution.py:271
  43.1 1.4 %shard_map.58 = (f32[1,128]{1,0:T(1,128)}, f32[1,128]{1,0:T(1,128)}, f32[64,128]{1,0:T(8,128)}, f32[64,128]{1,0:T(8,128)}) custom-call(f32[1,128]{1,0:T(1,128)} %get-tuple-element.12.refs_0_, f32[1,128]{1,0:T(1,128)} %get-tuple-element.13.refs_1_, f32[64,128]{1,0:T(8,128)} %get-tuple-element.14.refs_2_, f32[64,128]{1,0:T(8,128)} %get-tuple-element.15.refs_3_), custom_call_target="tpu_custom_call" | custom-call | tf_op jit(solution)/shard_map/pallas_call | solution.py:306

commit v3 on v2

--- a/solution.py
+++ b/solution.py
@@ -41,7 +41,6 @@
     f_out,
     f_in,
     f_all,
-    g_out,
     g_in,
     w_out,
     w_in,
@@ -69,8 +68,28 @@
     def src_peer(k):
         return {"rows": a * src + lax.rem(b + k, src)}
 
+    pairs = tgt & (tgt - 1) == 0
+
+    def chip(k):
+        if not pairs:
+            return lax.rem(a + tgt - k, tgt)
+        other, bit = a, 1
+        while bit <= k:
+            if k & bit:
+                other = other + bit * (1 - 2 * lax.rem(lax.div(a, bit), 2))
+            bit *= 2
+        return other
+
     def tgt_peer(k):
-        return {"rows": lax.rem(a + k, tgt) * src + b}
+        return {"rows": (chip(k) if pairs else lax.rem(a + k, tgt)) * src + b}
+
+    def chip_slot(c):
+        if not pairs:
+            return lax.rem(a + tgt - c, tgt)
+        return chip(c)
+
+    def core(p):
+        return lax.rem(b + src - p, src)
 
     local_s = pltpu.make_async_copy(s_hbm, s_all.at[0, 0], local_sem.at[0])
     local_t = pltpu.make_async_copy(t_hbm, t_all.at[0], local_sem.at[1])
@@ -95,11 +114,12 @@
         return copy
 
     t_copies, s_copies = {}, {}
-    for k in range(max(src, tgt) - 1, 0, -1):
-        if k < tgt:
+    far = tgt // 2
+    for k in range(1, src):
+        s_copies[k] = send(s_hbm, s_all.at[k, 0], point_send.at[0, k], point_recv.at[0, k], src_peer(k))
+    for k in list(range(far, tgt)) + list(range(1, far)):
+        if k:
             t_copies[k] = send(t_hbm, t_all.at[k], point_send.at[1, k], point_recv.at[1, k], tgt_peer(k))
-        if k < src:
-            s_copies[k] = send(s_hbm, s_all.at[k, 0], point_send.at[0, k], point_recv.at[0, k], src_peer(k))
 
     eye = lax.broadcasted_iota(jnp.int32, (n, n), 0) == lax.broadcasted_iota(jnp.int32, (n, n), 1)
 
@@ -114,13 +134,20 @@
     for k in range(1, src):
         s_copies[k].wait_recv()
     lefts = jnp.concatenate([(s_all[p, 0] * (2.0 * scale)).T for p in range(src)], axis=0)
-    g_rows = []
+    rows_of = lax.broadcasted_iota(jnp.int32, (tgt, n), 0)
+    g_hat = jnp.zeros((tgt, n), jnp.float32)
     for q in range(tgt):
         if q:
             t_copies[q].wait_recv()
         t = t_all[q]
-        g_rows.append(-scale * jnp.sum(t * t, axis=0, keepdims=True))
-        cross[:, q * n : (q + 1) * n] = jnp.dot(lefts, t, precision=HIGHEST, preferred_element_type=jnp.float32)
+        g_hat = jnp.where(rows_of == chip(q), -scale * jnp.sum(t * t, axis=0, keepdims=True), g_hat)
+        piece = jnp.dot(lefts, t, precision=HIGHEST, preferred_element_type=jnp.float32)
+        columns = pl.ds(pl.multiple_of(chip(q) * n, n), n)
+        for p in range(src):
+            cross[pl.ds(pl.multiple_of(core(p) * n, n), n), columns] = piece[p * n : (p + 1) * n]
+
+    def wide_row(rows):
+        return jnp.concatenate([rows[q : q + 1] for q in range(tgt)], axis=1)
 
     def row_weights(p, g_row):
         x = cross[p * n : (p + 1) * n, :] + g_row
@@ -139,7 +166,6 @@
     batches = [list(range(1, tgt))[i :: ITERS - 1] for i in range(ITERS - 1)]
     arriving, handed = {}, []
     f_hat = None
-    g_hat = None
     for it in range(ITERS):
         last = it == ITERS - 1
         if it:
@@ -152,7 +178,7 @@
         if not last:
             for k in batches[it]:
                 arriving[k] = send(s_hbm, s_all.at[0, k], b_send.at[k], b_recv.at[k], tgt_peer(k))
-        g_row = jnp.concatenate(g_rows, axis=1)
+        g_row = wide_row(g_hat)
         copies = []
         for p in range(src):
             top, w, total = row_weights(p, g_row)
@@ -160,9 +186,8 @@
             f_out[it, p] = part
             f_in[it, p, 0] = part
             for k in range(1, src):
-                to = (p + k) % src
                 copies.append(
-                    (to, send(f_out.at[it, p], f_in.at[it, to, k], f_send.at[it, to, k], f_recv.at[it, to, k], src_peer(k)))
+                    (p, send(f_out.at[it, p], f_in.at[it, p, k], f_send.at[it, p, k], f_recv.at[it, p, k], src_peer(k)))
                 )
         f_hat = []
         tops, totals = [], []
@@ -171,12 +196,13 @@
                 if to == p:
                     copy.wait_recv()
             f_hat.append(-(log_count + lse2(f_in[it, p])))
-            if last:
-                f_all[0, p] = f_hat[p]
             x = cross[p * n : (p + 1) * n, :] + to_col(f_hat[p])
             tops.append(jnp.max(x, axis=0, keepdims=True))
             totals.append(jnp.sum(jnp.exp2(x - tops[p]), axis=0, keepdims=True))
         if last:
+            f_mine = sum(jnp.where(b == p, f_hat[p], 0.0) for p in range(src))
+            for p in range(src):
+                f_all[0, p] = f_hat[p]
             f_copies = [
                 send(f_all.at[0], f_all.at[k], b_send.at[tgt + k], b_recv.at[tgt + k], tgt_peer(k))
                 for k in range(1, tgt)
@@ -185,13 +211,9 @@
         total = sum(totals[p] * jnp.exp2(tops[p] - top) for p in range(src))
         part = top + jnp.log2(total)
         for q in range(tgt):
-            piece = part[:, q * n : (q + 1) * n]
-            g_out[it, q] = piece
-            g_out[it, tgt + q] = piece
-            g_in[it, 0, q] = piece
+            g_in[it, 0, q : q + 1] = part[:, q * n : (q + 1) * n]
         copies = [
-            send(g_out.at[it, pl.ds(tgt - k, tgt)], g_in.at[it, k], g_send.at[it, k], g_recv.at[it, k], tgt_peer(k))
-            for k in range(1, tgt)
+            send(g_in.at[it, 0], g_in.at[it, k], g_send.at[it, k], g_recv.at[it, k], tgt_peer(k)) for k in range(1, tgt)
         ]
         if it == 0:
             for p in range(src):
@@ -206,13 +228,15 @@
         for copy in copies:
             copy.wait_recv()
         g_hat = -(log_count + lse2(g_in[it]))
-        g_rows = [g_hat[q] for q in range(tgt)]
-
-    g_row = jnp.concatenate(g_rows, axis=1)
-    rights = jnp.concatenate([t_all[q] for q in range(tgt)], axis=1)
+
+    g_row = wide_row(g_hat)
+    rights = jnp.concatenate([t_all[chip_slot(q)] for q in range(tgt)], axis=1)
     w_copies = []
     for p in list(range(1, src)) + [0]:
-        top, w, total = row_weights(p, g_row)
+        x = cross[pl.ds(pl.multiple_of(core(p) * n, n), n), :] + g_row
+        top = jnp.max(x, axis=1, keepdims=True)
+        w = jnp.exp2(x - top)
+        total = jnp.sum(w, axis=1, keepdims=True)
         mean = lax.dot_general(
             rights, w, (((1,), (1,)), ((), ())), precision=HIGHEST, preferred_element_type=jnp.float32
         )
@@ -223,14 +247,19 @@
 
     s = s_all[0, 0]
     t = t_all[0]
-    f_ref[...] = (f_hat[0] + scale * jnp.sum(s * s, axis=0, keepdims=True)) * (SOFTNESS * LN2)
-    g_ref[...] = (g_hat[0] + scale * jnp.sum(t * t, axis=0, keepdims=True)) * (SOFTNESS * LN2)
+    g_mine = jnp.sum(jnp.where(rows_of == a, g_hat, 0.0), axis=0, keepdims=True)
+    f_ref[...] = (f_mine + scale * jnp.sum(s * s, axis=0, keepdims=True)) * (SOFTNESS * LN2)
+    g_ref[...] = (g_mine + scale * jnp.sum(t * t, axis=0, keepdims=True)) * (SOFTNESS * LN2)
 
     for copy in f_copies:
         copy.wait_recv()
+
+    def f_slot(p, k):
+        return sum(jnp.where(core(p) == c, f_all[k, c], 0.0) for c in range(src))
+
     slots = [(p, k) for p in range(src) for k in range(tgt)]
-    f_row = jnp.concatenate([f_all[k, p] for p, k in slots], axis=1)
-    w = jnp.exp2(own_cross[...] + f_row + to_col(g_hat[0] + log_count))
+    f_row = jnp.concatenate([f_slot(p, k) for p, k in slots], axis=1)
+    w = jnp.exp2(own_cross[...] + f_row + to_col(g_mine + log_count))
     mean = lax.dot_general(
         jnp.concatenate([s_all[p, k] for p, k in slots], axis=1),
         w,
@@ -247,7 +276,7 @@
     mean = w_out[0, :feats, :] * jnp.exp2(parts[0] - row_lse)
     for p in range(1, src):
         mean = mean + w_in[p, :feats, :] * jnp.exp2(parts[p] - row_lse)
-    gs_ref[...] = jnp.exp2(f_hat[0] + row_lse + log_count) * (s - mean)
+    gs_ref[...] = jnp.exp2(f_mine + row_lse + log_count) * (s - mean)
 
     for copy in pending:
         copy.wait_send()
@@ -281,8 +310,7 @@
                 pltpu.VMEM((ITERS, src, 1, n), f32),
                 pltpu.VMEM((ITERS, src, src, 1, n), f32),
                 pltpu.VMEM((tgt, src, 1, n), f32),
-                pltpu.VMEM((ITERS, 2 * tgt, 1, n), f32),
-                pltpu.VMEM((ITERS, tgt, tgt, 1, n), f32),
+                pltpu.VMEM((ITERS, tgt, tgt, n), f32),
                 pltpu.VMEM((src, feats + 8, n), f32),
                 pltpu.VMEM((src, feats + 8, n), f32),
                 dma((2,)),

time: 44.8 us -> 44.9 us (level)
  no operation moved by 1% of the time
where the time goes in v3:
time: 44.9 us; the launch traced here: 44.7 us
  Pallas kernels  44 us (98%)
  between operations  0.64 us (1%)
    pallas_call x1, Pallas kernels, local(): pl.pallas_call(functools.partial(kernel, src, tgt), out_shape=(row, row,...  42.6 us
    pallas_call x1, Pallas kernels, local(): pl.pallas_call(hand_out, out_shape=(row, row, block, block))(f, g, gs, gt)  1.42 us

profile of v3, /device:TPU:0, one launch (start us, length us, event | category | flops | bytes accessed | tf_op | source)
XLA Modules:
  0.0 44.7 jit_solution(11660990759996942453)
XLA Ops:
  0.6 42.6 %shard_map.57 = (f32[1,128]{1,0:T(1,128)}, f32[1,128]{1,0:T(1,128)}, f32[64,128]{1,0:T(8,128)}, f32[64,128]{1,0:T(8,128)}) custom-call(f32[64,128]{1,0:T(8,128)} %s_hbm.1, f32[64,128]{1,0:T(8,128)} %t_hbm.1), custom_call_target="tpu_custom_call" | custom-call | tf_op jit(solution)/shard_map/pallas_call | solution.py:300
  43.3 1.4 %shard_map.58 = (f32[1,128]{1,0:T(1,128)}, f32[1,128]{1,0:T(1,128)}, f32[64,128]{1,0:T(8,128)}, f32[64,128]{1,0:T(8,128)}) custom-call(f32[1,128]{1,0:T(1,128)} %get-tuple-element.12.refs_0_, f32[1,128]{1,0:T(1,128)} %get-tuple-element.13.refs_1_, f32[64,128]{1,0:T(8,128)} %get-tuple-element.14.refs_2_, f32[64,128]{1,0:T(8,128)} %get-tuple-element.15.refs_3_), custom_call_target="tpu_custom_call" | custom-call | tf_op jit(solution)/shard_map/pallas_call | solution.py:334

commit v4 on v3

--- a/solution.py
+++ b/solution.py
@@ -213,7 +213,8 @@
         for q in range(tgt):
             g_in[it, 0, q : q + 1] = part[:, q * n : (q + 1) * n]
         copies = [
-            send(g_in.at[it, 0], g_in.at[it, k], g_send.at[it, k], g_recv.at[it, k], tgt_peer(k)) for k in range(1, tgt)
+            send(g_in.at[it, 0], g_in.at[it, k], g_send.at[it, k], g_recv.at[it, k], tgt_peer(k))
+            for k in range(tgt - 1, 0, -1)
         ]
         if it == 0:
             for p in range(src):

time: 44.9 us -> 44.1 us (0.982)
  Pallas kernels: 44 us -> 43.3 us
    pallas_call x1, Pallas kernels: 42.6 us -> 41.8 us  [local(): pl.pallas_call(functools.partial(kernel, src, tgt), out_shape=(row, row,...]
where the time goes in v4:
time: 44.1 us; the launch traced here: 43.9 us
  Pallas kernels  43.3 us (98%)
  between operations  0.64 us (1%)
    pallas_call x1, Pallas kernels, local(): pl.pallas_call(functools.partial(kernel, src, tgt), out_shape=(row, row,...  41.8 us
    pallas_call x1, Pallas kernels, local(): pl.pallas_call(hand_out, out_shape=(row, row, block, block))(f, g, gs, gt)  1.42 us

profile of v4, /device:TPU:0, one launch (start us, length us, event | category | flops | bytes accessed | tf_op | source)
XLA Modules:
  0.0 43.9 jit_solution(3573217327031366758)
XLA Ops:
  0.6 41.8 %shard_map.57 = (f32[1,128]{1,0:T(1,128)}, f32[1,128]{1,0:T(1,128)}, f32[64,128]{1,0:T(8,128)}, f32[64,128]{1,0:T(8,128)}) custom-call(f32[64,128]{1,0:T(8,128)} %s_hbm.1, f32[64,128]{1,0:T(8,128)} %t_hbm.1), custom_call_target="tpu_custom_call" | custom-call | tf_op jit(solution)/shard_map/pallas_call | solution.py:301
  42.5 1.4 %shard_map.58 = (f32[1,128]{1,0:T(1,128)}, f32[1,128]{1,0:T(1,128)}, f32[64,128]{1,0:T(8,128)}, f32[64,128]{1,0:T(8,128)}) custom-call(f32[1,128]{1,0:T(1,128)} %get-tuple-element.12.refs_0_, f32[1,128]{1,0:T(1,128)} %get-tuple-element.13.refs_1_, f32[64,128]{1,0:T(8,128)} %get-tuple-element.14.refs_2_, f32[64,128]{1,0:T(8,128)} %get-tuple-element.15.refs_3_), custom_call_target="tpu_custom_call" | custom-call | tf_op jit(solution)/shard_map/pallas_call | solution.py:335
